TPU v7x, 32 devices: a whole 2x2x4 slice. The times are simulated.
32 devices in a mesh: groups: 2 (over x), rows: 16 (over z, y, core).
Axes of the slice: x: 2, y: 2, z: 4, core: 2. Of those that a mesh axis runs over, the one named last changes fastest.
Arguments:
- samples: bfloat16 [32768, 256], P(('groups', 'rows')), parts along dimension 0
- omega_diag: float32 [256, 128, 128], P(('groups', 'rows')), parts along dimension 0, as said below
- omega_off: float32 [960, 128, 128], P(('groups', 'rows')), parts along dimension 0, as said below
- pattern: int32 [960, 2], P(('groups', 'rows')), parts along dimension 0, may hold values from 0 to 127, as said below
- block_count: int32 [256], P(('groups', 'rows')), parts along dimension 0, may hold values from 0 to 15, as said below
- diag_term: float32 [32768], P(('groups', 'rows')), parts along dimension 0, may hold values from -1 to -0.5
Outputs:
- omega_diag_next: float32 [256, 128, 128], P(('groups', 'rows')), parts along dimension 0
- omega_off_next: float32 [960, 128, 128], P(('groups', 'rows')), parts along dimension 0
- objective: float32 [2], P('groups'), parts along dimension 0
There are 2 independent parts, one for each index of `groups`. A program takes and returns all parts, laid end to end along the dimension named above; each array names one. Nothing has to cross between parts.
Inputs may be any that keep to these rules, and one draw needn't show every extreme that they name: `pattern`: row e names a stored off-diagonal block by its block row i, which lies on the device holding e, and its block column j; for live entries j lies on another device. A device's live entries come first, ordered by block row; the live entries of all devices are symmetric: (j, i) is live wherever (i, j) is, and no pair is named twice. Between the block rows of two devices there are either none or exactly 2 live blocks. Dead entries name the device's first block row twice. The live entries of a device are its first entries, as many as the sum of block_count over its 8 block rows; some device has all 30 entries live. `omega_diag`: each diagonal block is symmetric. Omega is symmetric: for live entries e = (i, j) and f = (j, i), omega_off[f] is the transpose of omega_off[e].
All inputs are finite; a program needn't handle non-finite values.
Results may differ from a plain program's by a relative error of at most 0.0003.
Values may be sent and summed in bfloat16 or wider, within the bound.
A program may use at most 128 MiB of HBM per device.

v0:
```python
import jax
import jax.numpy as jnp
from jax import lax
from jax.sharding import PartitionSpec as P

SLOTS = 2


STEP_SIZE = 0.5
PENALTY = 0.01


def soften(values, level):
    return values - jnp.clip(values, -level, level)


def scatter_rows(payload, targets, capacity):
    holder = jnp.zeros((capacity,) + payload.shape[1:], payload.dtype)
    return holder.at[targets].set(payload, mode="drop")


def shards(samples, omega_diag, omega_off, pattern, block_count, diag_term):
    devices = lax.axis_size("rows")
    position = lax.axis_index("rows")
    rows_dev = omega_diag.shape[0]
    block_edge = omega_diag.shape[1]
    samples_dev = samples.shape[1]
    entries = omega_off.shape[0]
    block_total = rows_dev * devices
    capacity = devices * SLOTS
    highest = lax.Precision.HIGHEST
    local_samples = samples.reshape(rows_dev, block_edge, samples_dev)
    entry_ids = jnp.arange(entries, dtype=jnp.int32)
    living = entry_ids < jnp.sum(block_count)
    row_glob = pattern[:, 0]
    col_glob = pattern[:, 1]
    row_local = row_glob - position * rows_dev
    owners = col_glob // rows_dev
    send_key = row_glob * block_total + col_glob
    back_key = col_glob * block_total + row_glob
    same_peer = (owners[:, None] == owners[None, :]) & living[None, :]
    send_rank = jnp.sum(same_peer & (send_key[None, :] < send_key[:, None]), axis=1)
    recv_rank = jnp.sum(same_peer & (back_key[None, :] < back_key[:, None]), axis=1)
    send_target = jnp.where(living, owners * SLOTS + send_rank, capacity)
    recv_source = jnp.where(living, owners * SLOTS + recv_rank, 0)
    masked = jnp.where(living[:, None, None], omega_off, 0.0)
    selector = (row_local[None, :] == jnp.arange(rows_dev, dtype=jnp.int32)[:, None]).astype(
        jnp.float32
    )
    arrived = lax.all_to_all(
        scatter_rows(local_samples[row_local], send_target, capacity).reshape(
            devices, SLOTS, block_edge, local_samples.shape[2]
        ),
        "rows",
        split_axis=0,
        concat_axis=0,
        tiled=True,
    )
    columns = local_samples.shape[2]
    fetched = arrived.reshape(capacity, block_edge, columns)[recv_source]
    projected = jnp.einsum(
        "kab,kbn->kan",
        omega_diag,
        local_samples,
        precision=highest,
        preferred_element_type=jnp.float32,
    )
    contributions = jnp.einsum(
        "eab,ebn->ean", masked, fetched, precision=highest, preferred_element_type=jnp.float32
    )
    projected = projected + jnp.einsum("re,ean->ran", selector, contributions, precision=highest)
    off_part = jnp.einsum(
        "ean,ebn->eab",
        projected[row_local],
        fetched,
        precision=highest,
        preferred_element_type=jnp.float32,
    )
    diag_part = jnp.einsum(
        "kan,kbn->kab",
        projected,
        local_samples,
        precision=highest,
        preferred_element_type=jnp.float32,
    )
    squares = jnp.sum(projected * projected)
    flipped_out = scatter_rows(jnp.swapaxes(off_part, 1, 2), send_target, capacity).reshape(
        devices, SLOTS, block_edge, block_edge
    )
    returned = lax.all_to_all(flipped_out, "rows", split_axis=0, concat_axis=0, tiled=True)
    mirrored = returned.reshape(capacity, block_edge, block_edge)[recv_source]
    gradient = (off_part + mirrored) / (2.0 * samples_dev)
    off_next = jnp.where(
        living[:, None, None], soften(omega_off - STEP_SIZE * gradient, STEP_SIZE * PENALTY), 0.0
    )
    identity = jnp.eye(block_edge, dtype=jnp.float32)[None]
    diag_gradient = (diag_part + jnp.swapaxes(diag_part, 1, 2)) / (
        2.0 * samples_dev
    ) + identity * diag_term.reshape(rows_dev, block_edge)[:, :, None]
    moved = omega_diag - STEP_SIZE * diag_gradient
    diag_next = jnp.where(identity > 0.5, moved, soften(moved, STEP_SIZE * PENALTY))
    local_term = squares / (2.0 * samples_dev) - jnp.sum(
        jnp.log(jnp.diagonal(omega_diag, axis1=1, axis2=2))
    )
    total_term = lax.psum(local_term, "rows")
    objective = (total_term / (block_total * block_edge)).reshape(1)
    return (diag_next, off_next, objective)


def solution(mesh):
    return jax.shard_map(
        shards,
        mesh=mesh,
        in_specs=(
            P(("groups", "rows"), None),
            P(("groups", "rows"), None, None),
            P(("groups", "rows"), None, None),
            P(("groups", "rows"), None),
            P(("groups", "rows")),
            P(("groups", "rows")),
        ),
        out_specs=(
            P(("groups", "rows"), None, None),
            P(("groups", "rows"), None, None),
            P("groups"),
        ),
        check_vma=False,
    )
```

profile of v0, /device:TPU:0, one launch (start us, length us, event | category | flops | bytes accessed | tf_op | source)
XLA Modules:
  0.0 179.7 jit_solution(3447105092942988332)
XLA Ops:
  0.6 0.8 fusion.16
  1.4 0.8 bitcast_subtract_fusion
  2.2 1.3 reduce_sum.49
  3.5 0.6 iota_compare_fusion.2
  4.2 0.2 convert_reduce_fusion
  4.3 0.7 fusion.17
  5.0 0.7 gather_fusion
  5.7 1.6 broadcast_in_dim.60
  7.3 5.3 %scatter_fusion = bf16[32,128,256]{2,1,0:T(8,128)(2,1)} fusion(bf16[32,128,256]{2,1,0:T(8,128)(2,1)} %broadcast_in_dim.60, s32[30]{0:T(128)S(1)} %get-tuple-element.14, bf16[30,128,256]{2,1,0:T(8,128)(2,1)S(1)} %gather_fusion), kind=kCustom, calls=%fused_computation.5 | custom fusion | bytes 5898360 | tf_op jit(solution)/shard_map/scatter | solution.py:19
  12.6 7.6 %all-to-all-start = ((bf16[16,2,128,256]{3,2,1,0:T(8,128)(2,1)}), bf16[16,2,128,256]{3,2,1,0:T(8,128)(2,1)S(1)}, u32[]{:S(2)}, u32[]{:S(2)}) async-start(bf16[16,2,128,256]{3,2,1,0:T(8,128)(2,1)} %bitcast.9), calls=%async_computation | async-start | bytes 4194304 | tf_op jit(solution)/shard_map/all_to_all | solution.py:50
  20.2 41.1 %all-to-all-done = bf16[16,2,128,256]{3,2,1,0:T(8,128)(2,1)S(1)} async-done(((bf16[16,2,128,256]{3,2,1,0:T(8,128)(2,1)}), bf16[16,2,128,256]{3,2,1,0:T(8,128)(2,1)S(1)}, u32[]{:S(2)}, u32[]{:S(2)}) %all-to-all-start) | async-done | bytes 2097184 | tf_op jit(solution)/shard_map/all_to_all | solution.py:50
  61.3 1.3 copy-done.2
  62.6 2.3 %gather_fusion.1 = bf16[30,128,256]{2,1,0:T(8,128)(2,1)S(1)} fusion(bf16[32,128,256]{2,1,0:T(8,128)(2,1)} %bitcast.76, s32[1024]{0:T(1024)S(1)} %pad_clamp_fusion), kind=kCustom, calls=%fused_computation.1 | custom fusion | bytes 3932280 | tf_op jit(solution)/shard_map/gather | solution.py:60
  64.9 4.2 %fusion.3 = f32[30,128,256]{2,1,0:T(8,128)S(1)} fusion(bf16[30,128,256]{2,1,0:T(8,128)(2,1)S(1)} %gather_fusion.1, f32[30,128,128]{2,1,0:T(8,128)} %param.8, pred[30]{0:T(512)(128)(4,1)S(1)} %iota_compare_fusion.2), kind=kOutput, calls=%fused_computation.11 | convolution fusion | flops 1510440960 | bytes 7864350 | tf_op jit(solution)/shard_map/eab,ebn->ean/dot_general | solution.py:68
  69.1 3.7 %fusion = f32[8,128,256]{2,0,1:T(8,128)S(1)} fusion(f32[30,128,256]{2,1,0:T(8,128)S(1)} %fusion.3, s32[30]{0:T(128)S(1)} %get-tuple-element.5), kind=kOutput, calls=%fused_computation.7 | convolution fusion | flops 94372080 | bytes 4980856 | tf_op jit(solution)/shard_map/re,ean->ran/dot_general | solution.py:71
  72.8 1.6 multiply_reduce_fusion
  74.4 2.7 %gather_fusion.2 = f32[30,128,256]{2,1,0:T(8,128)} fusion(f32[8,128,256]{2,1,0:T(8,128)S(1)} %get-tuple-element.16, s32[1024]{0:T(1024)S(1)} %pad_clamp_fusion.1), kind=kCustom, calls=%fused_computation.2 | custom fusion | bytes 7864440 | tf_op jit(solution)/shard_map/gather | solution.py:74
  77.1 4.6 %fusion.21 = f32[30,128,128]{2,1,0:T(8,128)S(1)} fusion(f32[30,128,256]{2,1,0:T(8,128)} %gather_fusion.2, bf16[30,128,256]{2,1,0:T(8,128)(2,1)} %copy-done.1), kind=kOutput, calls=%fused_computation.65 | convolution fusion | flops 1509949440 | bytes 7864320 | tf_op jit(solution)/shard_map/ean,ebn->eab/dot_general | solution.py:72
  81.7 1.8 copy.15
  83.5 1.5 broadcast_in_dim.62
  85.1 6.1 %scatter_fusion.1 = f32[32,128,128]{2,1,0:T(8,128)} fusion(f32[32,128,128]{2,1,0:T(8,128)} %broadcast_in_dim.62, s32[30]{0:T(128)S(1)} %get-tuple-element.14, f32[30,128,128]{2,1,0:T(8,128)} %copy.15), kind=kCustom, calls=%fused_computation.6 | custom fusion | bytes 5898360 | tf_op jit(solution)/shard_map/scatter | solution.py:19
  91.2 11.2 %all-to-all-start.1 = ((f32[16,2,128,128]{3,2,1,0:T(8,128)}), f32[16,2,128,128]{3,2,1,0:T(8,128)}, u32[]{:S(2)}, u32[]{:S(2)}) async-start(f32[16,2,128,128]{3,2,1,0:T(8,128)} %bitcast.74), calls=%async_computation.1 | async-start | bytes 4194304 | tf_op jit(solution)/shard_map/all_to_all | solution.py:90
  102.4 5.9 %copy.16 = f32[8,128,128]{0,2,1:T(8,128)} copy(f32[8,128,128]{2,1,0:T(8,128)} %param.7) | data formatting | bytes 1048576 | tf_op args[1]
  108.3 2.4 %gather_fusion.4 = f32[128,8]{1,0:T(8,128)} fusion(f32[8,128,128]{0,2,1:T(8,128)} %copy.16, s32[128]{0:T(128)S(1)} %or_bitcast_fusion), kind=kCustom, calls=%fused_computation.4 | custom fusion | bytes 9216 | tf_op jit(solution)/shard_map/jit(diagonal)/gather | solution.py:103
  110.7 1.5 log_reduce_fusion
  113.5 0.6 fusion.11
  114.1 51.2 %psum.7 = f32[]{:T(128)} all-reduce(f32[]{:T(128)S(6)} %sub.46), channel_id=1, replica_groups=mesh['groups'=2,'rows'=16] {'rows'}, use_global_device_ids=true, to_apply=%region_7.8 | all-reduce | flops 1 | bytes 8 | tf_op jit(solution)/shard_map/psum | solution.py:105
  165.3 1.4 fusion.20
  166.7 1.2 copy.14
  168.6 2.2 %subtract_select_fusion = f32[8,128,128]{2,1,0:T(8,128)} fusion(f32[8,128,128]{2,1,0:T(8,128)} %param.7, f32[8,128,128]{2,1,0:T(8,128)} %fusion.20, f32[8,128,128]{1,2,0:T(8,128)S(1)} %copy.14, f32[8,128]{1,0:T(8,128)} %bitcast.78, f32[128,128]{1,0:T(8,128)} %get-tuple-element.17, pred[128,128]{1,0:T(8,128)(4,1)S(1)} %get-tuple-element.18), kind=kLoop, calls=%fused_computation.17 | loop fusion | flops 1179648 | bytes 2183168 | tf_op jit(solution)/shard_map/jit(_where)/select_n | solution.py:101
  170.8 3.7 %gather_fusion.3 = f32[30,128,128]{2,1,0:T(8,128)} fusion(f32[32,128,128]{2,1,0:T(8,128)} %bitcast.18, s32[1024]{0:T(1024)} %copy-done.4), kind=kCustom, calls=%fused_computation.3 | custom fusion | bytes 3932280 | tf_op jit(solution)/shard_map/gather | solution.py:91
  174.5 4.1 %fusion.2 = f32[30,128,128]{2,1,0:T(8,128)} fusion(f32[30,128,128]{2,1,0:T(8,128)} %param.8, f32[30,128,128]{2,1,0:T(8,128)S(1)} %fusion.21, f32[30,128,128]{2,1,0:T(8,128)} %gather_fusion.3, pred[30]{0:T(512)(128)(4,1)S(1)} %copy-done.6), kind=kLoop, calls=%fused_computation.10 | loop fusion | flops 2949120 | bytes 7864350 | tf_op jit(solution)/shard_map/jit(_where)/select_n | solution.py:93
  (17 shorter events, 0.1 us)
Async XLA Ops:
  0.6 4.4 %copy-start = (bf16[1024,256]{1,0:T(8,128)(2,1)S(1)}, bf16[1024,256]{1,0:T(8,128)(2,1)}, u32[]{:S(2)}) copy-start(bf16[1024,256]{1,0:T(8,128)(2,1)} %param.6) | copy-start | bytes 1572868
  4.1 60.8 %copy-start.5 = (pred[30]{0:T(512)(128)(4,1)}, pred[30]{0:T(512)(128)(4,1)S(1)}, u32[]{:S(2)}) copy-start(pred[30]{0:T(512)(128)(4,1)S(1)} %iota_compare_fusion.2) | copy-start | bytes 94
  12.6 48.7 %all-to-all-start = ((bf16[16,2,128,256]{3,2,1,0:T(8,128)(2,1)}), bf16[16,2,128,256]{3,2,1,0:T(8,128)(2,1)S(1)}, u32[]{:S(2)}, u32[]{:S(2)}) async-start(bf16[16,2,128,256]{3,2,1,0:T(8,128)(2,1)} %bitcast.9), calls=%async_computation | async-start | bytes 4194304 | tf_op jit(solution)/shard_map/all_to_all | solution.py:50
  20.2 48.9 %copy-start.4 = (s32[1024]{0:T(1024)}, s32[1024]{0:T(1024)S(1)}, u32[]{:S(2)}) copy-start(s32[1024]{0:T(1024)S(1)} %pad_clamp_fusion) | copy-start | bytes 12292
  61.3 1.4 copy-start.2
  64.9 4.2 %copy-start.1 = (bf16[30,128,256]{2,1,0:T(8,128)(2,1)}, bf16[30,128,256]{2,1,0:T(8,128)(2,1)S(1)}, u32[]{:S(2)}) copy-start(bf16[30,128,256]{2,1,0:T(8,128)(2,1)S(1)} %gather_fusion.1) | copy-start | bytes 5898244
  69.1 3.7 %copy-start.3 = (f32[8,128,128]{2,1,0:T(8,128)S(1)}, f32[8,128,128]{2,1,0:T(8,128)}, u32[]{:S(2)}) copy-start(f32[8,128,128]{2,1,0:T(8,128)} %param.7) | copy-start | bytes 1572868
  91.2 79.7 %all-to-all-start.1 = ((f32[16,2,128,128]{3,2,1,0:T(8,128)}), f32[16,2,128,128]{3,2,1,0:T(8,128)}, u32[]{:S(2)}, u32[]{:S(2)}) async-start(f32[16,2,128,128]{3,2,1,0:T(8,128)} %bitcast.74), calls=%async_computation.1 | async-start | bytes 4194304 | tf_op jit(solution)/shard_map/all_to_all | solution.py:90
  170.8 3.7 %copy-start.6 = (pred[30]{0:T(512)(128)(4,1)S(1)}, pred[30]{0:T(512)(128)(4,1)}, u32[]{:S(2)}) copy-start(pred[30]{0:T(512)(128)(4,1)} %copy-done.5) | copy-start | bytes 94
where the time goes:
time: 183 us; the launch traced here: 180 us
  blocking collectives  51.2 us (28%)
  waiting for transfers between devices  41.1 us (22%)
  local copies, waits for them, and re-layouts  36.5 us (20%)
  starting transfers between devices  18.8 us (10%)
  matrix products  15.5 us (8%)
  other arithmetic  12.7 us (7%)
  between operations  3.89 us (2%)
    psum x1, blocking collectives, shards(): total_term = lax.psum(local_term, 'rows')  51.2 us
    all_to_all x1, waiting for transfers between devices, shards(): lax.all_to_all(scatter_rows(local_samples[row_local], send_target, capaci...  41.1 us
    scatter x2, local copies, waits for them, and re-layouts, scatter_rows(): return holder.at[targets].set(payload, mode='drop')  11.4 us
    all_to_all x1, starting transfers between devices, shards(): lax.all_to_all(flipped_out, 'rows', split_axis=0, concat_axis=0, tiled=True)  11.2 us
    all_to_all x1, starting transfers between devices, shards(): lax.all_to_all(scatter_rows(local_samples[row_local], send_target, capaci...  7.57 us
    unnamed x15, local copies, waits for them, and re-layouts  7.25 us
    dot_general x1, matrix products, shards(): jnp.einsum('ean,ebn->eab', projected[row_local], fetched, precision=highe...  4.62 us
    dot_general x1, matrix products, shards(): jnp.einsum('eab,ebn->ean', masked, fetched, precision=highest, preferred_...  4.17 us
  transfers between devices with their start and end apart: 2, of which 1 were waited for; matrix products, arithmetic and copies ran while one was open for 8% of the time, Pallas kernels for 0%

commit v1 on v0

v1 whole, which is shorter than its diff:
```python
import functools

import jax
import jax.numpy as jnp
from jax import lax
from jax.experimental import pallas as pl
from jax.experimental.pallas import tpu as pltpu
from jax.sharding import PartitionSpec as P

STEP_SIZE = 0.5
PENALTY = 0.01
LEVELS = 32767.0
AXIS = "rows"


def soften(values, level):
    return values - jnp.clip(values, -level, level)


def halves(values):
    high = values.astype(jnp.bfloat16)
    low = (values - high.astype(jnp.float32)).astype(jnp.bfloat16)
    return jnp.concatenate([high, low], axis=1)


def times(left, right):
    return lax.dot_general(
        halves(left),
        jnp.concatenate([right, right], axis=0),
        (((1,), (0,)), ((), ())),
        preferred_element_type=jnp.float32,
    )


def times_turned(left, right):
    return lax.dot_general(
        halves(left),
        jnp.concatenate([right, right], axis=1),
        (((1,), (1,)), ((), ())),
        preferred_element_type=jnp.float32,
    )


def peer_of(me, step, n):
    if n & (n - 1):
        return (me + step) % n
    total = 0
    bit = 1
    while bit < n:
        total = total + bit * (((me // bit) % 2 + (step // bit) % 2) % 2)
        bit *= 2
    return total


def kernel(
    n,
    table,
    pattern,
    counts,
    samples,
    diag_hbm,
    off_hbm,
    term,
    diag_out,
    off_out,
    objective,
    diag,
    off,
    x_send,
    x_recv,
    parts,
    runs,
    q_send,
    q_recv,
    aux_send,
    aux_recv,
    last,
    logs,
    load_sems,
    out_sems,
    x_send_sems,
    x_recv_sems,
    q_send_sems,
    q_recv_sems,
    aux_send_sems,
    aux_recv_sems,
):
    me = lax.axis_index(AXIS)
    rows, edge = diag.shape[0], diag.shape[1]
    entries = off.shape[0]
    columns = samples.shape[2]
    width = 2.0 * columns

    load_diag = pltpu.make_async_copy(diag_hbm, diag, load_sems.at[0])
    load_off = pltpu.make_async_copy(off_hbm, off, load_sems.at[1])
    load_diag.start()
    load_off.start()

    barrier = pltpu.get_barrier_semaphore()

    def greet(i, carry):
        pl.semaphore_signal(
            barrier,
            inc=1,
            device_id={AXIS: peer_of(me, n - 1 - i, n)},
            device_id_type=pl.DeviceIdType.MESH,
        )
        return carry

    lax.fori_loop(0, n - 1, greet, 0)

    def remote(source, target, send_sems, recv_sems, peer, mine):
        return pltpu.make_async_remote_copy(
            src_ref=source.at[peer],
            dst_ref=target.at[mine],
            send_sem=send_sems.at[peer],
            recv_sem=recv_sems.at[mine],
            device_id={AXIS: peer},
            device_id_type=pl.DeviceIdType.MESH,
        )

    x_copy = functools.partial(remote, x_send, x_recv, x_send_sems, x_recv_sems)
    q_copy = functools.partial(remote, q_send, q_recv, q_send_sems, q_recv_sems)
    aux_copy = functools.partial(
        remote, aux_send, aux_recv, aux_send_sems, aux_recv_sems
    )

    pl.semaphore_wait(barrier, n - 1)

    def send_samples(i, carry):
        peer = peer_of(me, n - 1 - i, n)
        for slot in range(2):
            entry = table[slot, peer]
            x_send[peer, slot] = samples[pattern[entry, 0] % rows]
        x_copy(peer, me).start()
        return carry

    lax.fori_loop(0, n - 1, send_samples, 0)

    eye = lax.broadcasted_iota(jnp.int32, (edge, edge), 0) == lax.broadcasted_iota(
        jnp.int32, (edge, edge), 1
    )
    identity = eye.astype(jnp.float32)

    total = jnp.int32(0)
    for r in range(rows):
        count = counts[r]
        total = total + count
        last[r] = jnp.where(count > 0, rows + total - 1, r)

    load_diag.wait()

    logs[...] = jnp.zeros_like(logs)

    def own_products(r, carry):
        block = diag[r]
        runs[r] = times(block, samples[r])
        logs[...] += jnp.log(jnp.sum(block * identity, axis=0, keepdims=True))
        return carry

    lax.fori_loop(0, rows, own_products, 0)
    load_off.wait()

    def take_samples(i, carry):
        peer = peer_of(me, n - 1 - i, n)
        x_copy(peer, peer).wait_recv()
        for slot in range(2):
            entry = table[2 + slot, peer]
            parts[peer, slot] = times(off[entry], x_recv[peer, slot])
        return carry

    lax.fori_loop(0, n - 1, take_samples, 0)

    def place(entry):
        owner = pattern[entry, 1] // rows
        return owner, jnp.where(table[3, owner] == entry, 1, 0)

    def accumulate(entry, carry):
        row = pattern[entry, 0] % rows
        before = pattern[jnp.maximum(entry - 1, 0), 0] % rows
        fresh = (entry == 0) | (row != before)
        base = jnp.where(fresh, row, rows + entry - 1)
        owner, slot = place(entry)
        part = parts[owner, slot]
        runs[rows + entry] = runs[base] + jnp.where(entry < total, part, 0.0)
        return carry

    lax.fori_loop(0, entries, accumulate, 0)

    squares = jnp.zeros((1, columns), jnp.float32)
    for r in range(rows):
        values = runs[last[r]]
        squares = squares + jnp.sum(values * values, axis=0, keepdims=True)
    lanes = -logs[...]
    for start in range(0, columns, edge):
        lanes = lanes + squares[:, start : start + edge] / width
    aux_recv[me, 2:3, :] = lanes

    def send_products(i, carry):
        peer = peer_of(me, n - 1 - i, n)
        for slot in range(2):
            entry = table[slot, peer]
            values = runs[last[pattern[entry, 0] % rows]]
            other = jnp.where(table[3, peer] == entry, 1, 0)
            product = times_turned(values, x_recv[peer, other])
            parts[peer, slot, :, :edge] = product
            largest = jnp.maximum(
                jnp.max(jnp.abs(product), axis=0, keepdims=True), 1e-30
            )
            coded = jnp.round(product * (LEVELS / largest))
            q_send[peer, slot] = coded.astype(jnp.int32).astype(jnp.int16)
            aux_send[peer, slot : slot + 1, :] = largest / LEVELS
        aux_send[peer, 2:3, :] = lanes
        aux_copy(peer, me).start()
        q_copy(peer, me).start()
        return carry

    lax.fori_loop(0, n - 1, send_products, 0)

    def finish_diag(r, carry):
        product = times_turned(runs[last[r]], samples[r])
        slope = (product + product.T) / width + identity * term[pl.ds(r, 1), :]
        moved = diag[r] - STEP_SIZE * slope
        diag_out[r] = jnp.where(eye, moved, soften(moved, STEP_SIZE * PENALTY))
        return carry

    lax.fori_loop(0, rows, finish_diag, 0)

    def take_products(i, carry):
        peer = peer_of(me, n - 1 - i, n)
        aux_copy(peer, peer).wait_recv()
        q_copy(peer, peer).wait_recv()
        for slot in range(2):
            entry = table[2 + slot, peer]
            sent = jnp.where(table[1, peer] == entry, 1, 0)
            product = parts[peer, sent][:, :edge]
            scale = aux_recv[peer, slot : slot + 1, :]
            coded = q_recv[peer, slot].astype(jnp.int32).astype(jnp.float32)
            slope = (product + (coded * scale).T) / width
            parts[peer, slot, :, edge : 2 * edge] = soften(
                off[entry] - STEP_SIZE * slope, STEP_SIZE * PENALTY
            )
        return carry

    lax.fori_loop(0, n - 1, take_products, 0)

    def store_copy(entry):
        return pltpu.make_async_copy(
            runs.at[rows + entry, :, pl.ds(0, edge)],
            off_out.at[entry],
            out_sems.at[entry],
        )

    def store_off(entry, carry):
        owner, slot = place(entry)
        values = parts[owner, slot][:, edge : 2 * edge]
        runs[rows + entry, :, :edge] = jnp.where(entry < total, values, 0.0)
        store_copy(entry).start()
        return carry

    lax.fori_loop(0, entries, store_off, 0)

    def add_lanes(d, carry):
        return carry + aux_recv[d, 2:3, :]

    lanes = lax.fori_loop(0, n, add_lanes, jnp.zeros((1, edge), jnp.float32))
    objective[...] = jnp.broadcast_to(
        jnp.sum(lanes, axis=1, keepdims=True) / (rows * n * edge), objective.shape
    )

    def drain(i, carry):
        peer = peer_of(me, n - 1 - i, n)
        x_copy(peer, me).wait_send()
        q_copy(peer, me).wait_send()
        aux_copy(peer, me).wait_send()
        return carry

    lax.fori_loop(0, n - 1, drain, 0)

    def drain_out(entry, carry):
        store_copy(entry).wait()
        return carry

    lax.fori_loop(0, entries, drain_out, 0)


def shards(samples, omega_diag, omega_off, pattern, block_count, diag_term):
    n = lax.axis_size(AXIS)
    rows, edge = omega_diag.shape[0], omega_diag.shape[1]
    columns = samples.shape[1]
    entries = omega_off.shape[0]
    blocks = rows * n
    ids = jnp.arange(entries, dtype=jnp.int32)
    living = ids < jnp.sum(block_count)
    row, col = pattern[:, 0], pattern[:, 1]
    forth = row * blocks + col
    back = col * blocks + row
    top = blocks * blocks
    keys = jnp.stack([forth, top - forth, back, top - back]) * entries + ids
    linked = living & (
        (col // rows)[None, :] == jnp.arange(n, dtype=jnp.int32)[:, None]
    )
    table = (
        jnp.min(
            jnp.where(linked[None], keys[:, None, :], (top + 1) * entries), axis=2
        )
        % entries
    )
    f32, bf16, i16 = jnp.float32, jnp.bfloat16, jnp.int16
    smem = pl.BlockSpec(memory_space=pltpu.SMEM)
    vmem = pl.BlockSpec(memory_space=pltpu.VMEM)
    hbm = pl.BlockSpec(memory_space=pl.ANY)
    dma = pltpu.SemaphoreType.DMA
    diag_next, off_next, objective = pl.pallas_call(
        functools.partial(kernel, n),
        out_shape=(
            jax.ShapeDtypeStruct(omega_diag.shape, f32),
            jax.ShapeDtypeStruct(omega_off.shape, f32),
            jax.ShapeDtypeStruct((1, edge), f32),
        ),
        in_specs=[smem, smem, smem, vmem, hbm, hbm, vmem],
        out_specs=(vmem, hbm, vmem),
        scratch_shapes=[
            pltpu.VMEM(omega_diag.shape, f32),
            pltpu.VMEM(omega_off.shape, f32),
            pltpu.VMEM((n, 2, edge, columns), bf16),
            pltpu.VMEM((n, 2, edge, columns), bf16),
            pltpu.VMEM((n, 2, edge, columns), f32),
            pltpu.VMEM((rows + entries, edge, columns), f32),
            pltpu.VMEM((n, 2, edge, edge), i16),
            pltpu.VMEM((n, 2, edge, edge), i16),
            pltpu.VMEM((n, 8, edge), f32),
            pltpu.VMEM((n, 8, edge), f32),
            pltpu.SMEM((rows,), jnp.int32),
            pltpu.VMEM((1, edge), f32),
            dma((2,)),
            dma((entries,)),
        ]
        + [dma((n,))] * 6,
        compiler_params=pltpu.CompilerParams(
            collective_id=0,
            has_side_effects=True,
            vmem_limit_bytes=60 * 1024 * 1024,
        ),
    )(
        table,
        pattern,
        block_count,
        samples.reshape(rows, edge, columns),
        omega_diag,
        omega_off,
        diag_term.reshape(rows, edge),
    )
    return diag_next, off_next, objective[0, :1]


def solution(mesh):
    return jax.shard_map(
        shards,
        mesh=mesh,
        in_specs=(
            P(("groups", "rows"), None),
            P(("groups", "rows"), None, None),
            P(("groups", "rows"), None, None),
            P(("groups", "rows"), None),
            P(("groups", "rows")),
            P(("groups", "rows")),
        ),
        out_specs=(
            P(("groups", "rows"), None, None),
            P(("groups", "rows"), None, None),
            P("groups"),
        ),
        check_vma=False,
    )
```

time: 183 us -> 98.9 us (0.54); the launches traced: 180 us -> 98.6 us
  Pallas kernels: 0 us -> 86.4 us
  blocking collectives: 51.2 us -> 0 us
  waiting for transfers between devices: 41.1 us -> 0 us
  local copies, waits for them, and re-layouts: 36.5 us -> 6.26 us
  starting transfers between devices: 18.8 us -> 0 us
  matrix products: 15.5 us -> 0 us
  other arithmetic: 12.7 us -> 4.16 us
  between operations: 3.89 us -> 1.82 us
    pallas_call x0 -> x1, Pallas kernels: none -> 86.4 us  [shards(): pl.pallas_call(functools.partial(kernel, n), out_shape=(jax.ShapeDtypeStr...]
    psum x1 -> x0, blocking collectives: 51.2 us -> none  [shards(): total_term = lax.psum(local_term, 'rows')]
    all_to_all x2 -> x0, waiting for transfers between devices: 41.1 us -> none  [the longest x1 41.1 us: shards(): lax.all_to_all(scatter_rows(local_samples[row_local], send_target, capaci...]
    all_to_all x2 -> x0, starting transfers between devices: 18.8 us -> none  [the longest x1 11.2 us: shards(): lax.all_to_all(flipped_out, 'rows', split_axis=0, concat_axis=0, tiled=True)]
    dot_general x5 -> x0, matrix products: 15.5 us -> none  [the longest x1 4.62 us: shards(): jnp.einsum('ean,ebn->eab', projected[row_local], fetched, precision=highe...]
    gather x5 -> x0, local copies, waits for them, and re-layouts: 11.7 us -> none  [the longest x1 3.66 us: shards(): mirrored = returned.reshape(capacity, block_edge, block_edge)[recv_source]]
    scatter x2 -> x0, local copies, waits for them, and re-layouts: 11.4 us -> none  [scatter_rows(): return holder.at[targets].set(payload, mode='drop')]
    select_n x4 -> x2, other arithmetic: 7.7 us -> 1.29 us  [the longest x1 0.69 us: shards(): col // rows]
  transfers between devices with their start and end apart: 2 -> 0, of which waited for: 1 -> 0; matrix products, arithmetic and copies ran while one was open for 8% -> 0% of each run, Pallas kernels for 0% -> 0%
where the time goes in v1:
time: 98.9 us; the launch traced here: 98.6 us
  Pallas kernels  86.4 us (87%)
  local copies, waits for them, and re-layouts  6.26 us (6%)
  other arithmetic  4.16 us (4%)
  between operations  1.82 us (2%)
    pallas_call x1, Pallas kernels, shards(): pl.pallas_call(functools.partial(kernel, n), out_shape=(jax.ShapeDtypeStr...  86.4 us
    unnamed x5, local copies, waits for them, and re-layouts  6.26 us

profile of v1, /device:TPU:0, one launch (start us, length us, event | category | flops | bytes accessed | tf_op | source)
XLA Modules:
  0.0 98.6 jit_solution(7796109177887674057)
XLA Ops:
  0.6 1.3 %reduce_sum.9 = s32[]{:T(128)} reduce(s32[8]{0:T(128)} %counts.1, s32[]{:T(128)} %constant.27.clone.1), dimensions={0}, to_apply=%region_0.0 | reduce | flops 7 | bytes 40 | tf_op jit(solution)/shard_map/reduce_sum | solution.py:294
  1.9 0.6 iota_compare_fusion.1
  2.6 0.7 and_select_fusion
  3.3 0.8 broadcast_subtract_fusion.1
  4.1 0.1 select_reduce_fusion
  4.2 0.6 add_select_fusion.table
  4.8 1.4 %copy.10.pattern = s32[30,2]{1,0:T(8,128)} copy(s32[30,2]{0,1:T(2,128)} %param.9) | data formatting | bytes 480 | tf_op args[3]
  6.2 86.4 %shard_map.85 = (f32[8,128,128]{2,1,0:T(8,128)}, f32[30,128,128]{2,1,0:T(8,128)}, f32[1,128]{1,0:T(1,128)}) custom-call(s32[4,16]{1,0:T(4,128)} %add_select_fusion.table, s32[30,2]{1,0:T(8,128)} %copy.10.pattern, s32[8]{0:T(128)} %counts.1, bf16[8,128,256]{2,1,0:T(8,128)(2,1)} %bitcast.26, f32[8,128,128]{2,1,0:T(8,128)} %diag_hbm.1, ...), custom_call_target="tpu_custom_call" | custom-call | tf_op jit(solution)/shard_map/pallas_call | solution.py:314
  92.6 1.9 %copy.14 = f32[8,128,128]{2,1,0:T(8,128)} copy(f32[8,128,128]{2,1,0:T(8,128)} %get-tuple-element.18) | data formatting | bytes 1048576
  94.5 0.0 copy-start
  94.5 3.0 %copy.15 = f32[30,128,128]{2,1,0:T(8,128)} copy(f32[30,128,128]{2,1,0:T(8,128)} %get-tuple-element.19) | data formatting | bytes 3932160
  97.5 0.0 copy-done
  (2 shorter events, 0.0 us)
Async XLA Ops:
  94.5 3.0 %copy-start = (f32[1,128]{1,0:T(1,128)S(1)}, f32[1,128]{1,0:T(1,128)}, u32[]{:S(2)}) copy-start(f32[1,128]{1,0:T(1,128)} %get-tuple-element.8) | copy-start | bytes 1540

commit v2 on v1

--- a/solution.py
+++ b/solution.py
@@ -54,8 +54,8 @@
 
 def kernel(
     n,
-    table,
     pattern,
+    pattern_rows,
     counts,
     samples,
     diag_hbm,
@@ -76,6 +76,8 @@
     aux_recv,
     last,
     logs,
+    table_rows,
+    table_smem,
     load_sems,
     out_sems,
     x_send_sems,
@@ -96,6 +98,28 @@
     load_diag.start()
     load_off.start()
 
+    row, col = pattern_rows[0:1, :], pattern_rows[1:2, :]
+    blocks = rows * n
+    forth, back, top = row * blocks + col, col * blocks + row, blocks * blocks
+    ids = lax.broadcasted_iota(jnp.int32, (1, entries), 1)
+    low = lax.broadcasted_iota(jnp.int32, (n, entries), 0) * rows
+    linked = (col >= low) & (col < low + rows)
+    lane = lax.broadcasted_iota(jnp.int32, table_rows.shape, 1)
+    found = jnp.zeros(table_rows.shape, jnp.int32)
+    for which, key in enumerate((forth, top - forth, back, top - back)):
+        least = jnp.min(
+            jnp.where(linked, key * entries + ids, (top + 1) * entries),
+            axis=1,
+            keepdims=True,
+        )
+        found = jnp.where(lane == which, least, found)
+    table_rows[...] = found
+    load_table = pltpu.make_async_copy(table_rows, table_smem, load_sems.at[2])
+    load_table.start()
+
+    def find(which, peer):
+        return table_smem[peer, which] % entries
+
     barrier = pltpu.get_barrier_semaphore()
 
     def greet(i, carry):
@@ -125,13 +149,14 @@
         remote, aux_send, aux_recv, aux_send_sems, aux_recv_sems
     )
 
+    load_table.wait()
     pl.semaphore_wait(barrier, n - 1)
 
     def send_samples(i, carry):
         peer = peer_of(me, n - 1 - i, n)
         for slot in range(2):
-            entry = table[slot, peer]
-            x_send[peer, slot] = samples[pattern[entry, 0] % rows]
+            entry = find(slot, peer)
+            x_send[peer, slot] = samples[pattern[0, entry] % rows]
         x_copy(peer, me).start()
         return carry
 
@@ -165,19 +190,19 @@
         peer = peer_of(me, n - 1 - i, n)
         x_copy(peer, peer).wait_recv()
         for slot in range(2):
-            entry = table[2 + slot, peer]
+            entry = find(2 + slot, peer)
             parts[peer, slot] = times(off[entry], x_recv[peer, slot])
         return carry
 
     lax.fori_loop(0, n - 1, take_samples, 0)
 
     def place(entry):
-        owner = pattern[entry, 1] // rows
-        return owner, jnp.where(table[3, owner] == entry, 1, 0)
+        owner = pattern[1, entry] // rows
+        return owner, jnp.where(find(3, owner) == entry, 1, 0)
 
     def accumulate(entry, carry):
-        row = pattern[entry, 0] % rows
-        before = pattern[jnp.maximum(entry - 1, 0), 0] % rows
+        row = pattern[0, entry] % rows
+        before = pattern[0, jnp.maximum(entry - 1, 0)] % rows
         fresh = (entry == 0) | (row != before)
         base = jnp.where(fresh, row, rows + entry - 1)
         owner, slot = place(entry)
@@ -199,9 +224,9 @@
     def send_products(i, carry):
         peer = peer_of(me, n - 1 - i, n)
         for slot in range(2):
-            entry = table[slot, peer]
-            values = runs[last[pattern[entry, 0] % rows]]
-            other = jnp.where(table[3, peer] == entry, 1, 0)
+            entry = find(slot, peer)
+            values = runs[last[pattern[0, entry] % rows]]
+            other = jnp.where(find(3, peer) == entry, 1, 0)
             product = times_turned(values, x_recv[peer, other])
             parts[peer, slot, :, :edge] = product
             largest = jnp.maximum(
@@ -231,8 +256,8 @@
         aux_copy(peer, peer).wait_recv()
         q_copy(peer, peer).wait_recv()
         for slot in range(2):
-            entry = table[2 + slot, peer]
-            sent = jnp.where(table[1, peer] == entry, 1, 0)
+            entry = find(2 + slot, peer)
+            sent = jnp.where(find(1, peer) == entry, 1, 0)
             product = parts[peer, sent][:, :edge]
             scale = aux_recv[peer, slot : slot + 1, :]
             coded = q_recv[peer, slot].astype(jnp.int32).astype(jnp.float32)
@@ -289,28 +314,15 @@
     rows, edge = omega_diag.shape[0], omega_diag.shape[1]
     columns = samples.shape[1]
     entries = omega_off.shape[0]
-    blocks = rows * n
-    ids = jnp.arange(entries, dtype=jnp.int32)
-    living = ids < jnp.sum(block_count)
-    row, col = pattern[:, 0], pattern[:, 1]
-    forth = row * blocks + col
-    back = col * blocks + row
-    top = blocks * blocks
-    keys = jnp.stack([forth, top - forth, back, top - back]) * entries + ids
-    linked = living & (
-        (col // rows)[None, :] == jnp.arange(n, dtype=jnp.int32)[:, None]
-    )
-    table = (
-        jnp.min(
-            jnp.where(linked[None], keys[:, None, :], (top + 1) * entries), axis=2
-        )
-        % entries
-    )
     f32, bf16, i16 = jnp.float32, jnp.bfloat16, jnp.int16
     smem = pl.BlockSpec(memory_space=pltpu.SMEM)
     vmem = pl.BlockSpec(memory_space=pltpu.VMEM)
     hbm = pl.BlockSpec(memory_space=pl.ANY)
     dma = pltpu.SemaphoreType.DMA
+    held = n * 2 * edge * (columns * 8 + edge * 4) + (
+        (rows + entries) * edge * columns + entries * edge * edge
+    ) * 4
+    held = held + rows * edge * (edge * 8 + columns * 2)
     diag_next, off_next, objective = pl.pallas_call(
         functools.partial(kernel, n),
         out_shape=(
@@ -318,7 +330,7 @@
             jax.ShapeDtypeStruct(omega_off.shape, f32),
             jax.ShapeDtypeStruct((1, edge), f32),
         ),
-        in_specs=[smem, smem, smem, vmem, hbm, hbm, vmem],
+        in_specs=[smem, vmem, smem, vmem, hbm, hbm, vmem],
         out_specs=(vmem, hbm, vmem),
         scratch_shapes=[
             pltpu.VMEM(omega_diag.shape, f32),
@@ -333,18 +345,20 @@
             pltpu.VMEM((n, 8, edge), f32),
             pltpu.SMEM((rows,), jnp.int32),
             pltpu.VMEM((1, edge), f32),
-            dma((2,)),
+            pltpu.VMEM((n, 128), jnp.int32),
+            pltpu.SMEM((n, 128), jnp.int32),
+            dma((3,)),
             dma((entries,)),
         ]
         + [dma((n,))] * 6,
         compiler_params=pltpu.CompilerParams(
             collective_id=0,
             has_side_effects=True,
-            vmem_limit_bytes=60 * 1024 * 1024,
+            vmem_limit_bytes=min(held + (4 << 20), 60 << 20),
         ),
     )(
-        table,
-        pattern,
+        pattern.T,
+        pattern.T,
         block_count,
         samples.reshape(rows, edge, columns),
         omega_diag,

time: 98.9 us -> 96 us (0.971)
  other arithmetic: 4.16 us -> 0 us
  local copies, waits for them, and re-layouts: 6.26 us -> 7.71 us
    unnamed x5 -> x14, local copies, waits for them, and re-layouts: 6.26 us -> 7.71 us
    reduce_sum x1 -> x0, other arithmetic: 1.29 us -> none  [shards(): living = ids < jnp.sum(block_count)]
    select_n x2 -> x0, other arithmetic: 1.29 us -> none  [the longest x1 0.69 us: shards(): col // rows]
where the time goes in v2:
time: 96 us; the launch traced here: 95.7 us
  Pallas kernels  86.2 us (90%)
  local copies, waits for them, and re-layouts  7.71 us (8%)
  between operations  1.82 us (2%)
    pallas_call x1, Pallas kernels, shards(): pl.pallas_call(functools.partial(kernel, n), out_shape=(jax.ShapeDtypeStr...  86.2 us
    unnamed x14, local copies, waits for them, and re-layouts  7.71 us

profile of v2, /device:TPU:0, one launch (start us, length us, event | category | flops | bytes accessed | tf_op | source)
XLA Modules:
  0.0 95.7 jit_solution(11472463992903551854)
XLA Ops:
  0.6 0.0 copy-start
  0.6 1.5 %copy-done = f32[30,128,128]{2,1,0:T(8,128)S(1)} copy-done((f32[30,128,128]{2,1,0:T(8,128)S(1)}, f32[30,128,128]{2,1,0:T(8,128)}, u32[]{:S(2)}) %copy-start) | copy-done | bytes 1966104
  2.2 0.0 copy-start.1
  2.2 1.0 %copy-done.1 = bf16[1024,256]{1,0:T(8,128)(2,1)S(1)} copy-done((bf16[1024,256]{1,0:T(8,128)(2,1)S(1)}, bf16[1024,256]{1,0:T(8,128)(2,1)}, u32[]{:S(2)}) %copy-start.1) | copy-done | bytes 524312
  3.2 0.0 copy-start.2
  3.2 1.0 %copy-done.2 = f32[8,128,128]{2,1,0:T(8,128)S(1)} copy-done((f32[8,128,128]{2,1,0:T(8,128)S(1)}, f32[8,128,128]{2,1,0:T(8,128)}, u32[]{:S(2)}) %copy-start.2) | copy-done | bytes 524312
  4.3 0.0 copy-start.3
  4.3 0.7 copy-done.3
  4.9 0.0 copy-start.4
  5.0 0.7 copy-done.4
  5.6 0.0 copy-start.5
  5.6 0.7 copy-done.5
  6.3 86.2 %shard_map.85 = (f32[8,128,128]{2,1,0:T(8,128)S(1)}, f32[30,128,128]{2,1,0:T(8,128)S(1)}, f32[1,128]{1,0:T(1,128)S(1)}) custom-call(s32[2,30]{1,0:T(2,128)S(1)} %bitcast.7, s32[2,30]{1,0:T(2,128)S(1)} %bitcast.8, s32[8]{0:T(128)S(1)} %copy-done.5, bf16[8,128,256]{2,1,0:T(8,128)(2,1)S(1)} %bitcast.5, f32[8,128,128]{2,1,0:T(8,128)S(1)} %copy-done.2, ...), custom_call_target="tpu_custom_call" | custom-call | tf_op jit(solution)/shard_map/pallas_call | solution.py:326
  92.5 0.8 copy.12
  93.3 1.3 %copy.13 = f32[30,128,128]{2,1,0:T(8,128)} copy(f32[30,128,128]{2,1,0:T(8,128)S(1)} %get-tuple-element.13) | data formatting | bytes 3932160
Async XLA Ops:
  0.6 1.5 %copy-start = (f32[30,128,128]{2,1,0:T(8,128)S(1)}, f32[30,128,128]{2,1,0:T(8,128)}, u32[]{:S(2)}) copy-start(f32[30,128,128]{2,1,0:T(8,128)} %off_hbm.1) | copy-start | bytes 5898244
  2.2 1.0 %copy-start.1 = (bf16[1024,256]{1,0:T(8,128)(2,1)S(1)}, bf16[1024,256]{1,0:T(8,128)(2,1)}, u32[]{:S(2)}) copy-start(bf16[1024,256]{1,0:T(8,128)(2,1)} %param.6) | copy-start | bytes 1572868
  3.2 1.0 %copy-start.2 = (f32[8,128,128]{2,1,0:T(8,128)S(1)}, f32[8,128,128]{2,1,0:T(8,128)}, u32[]{:S(2)}) copy-start(f32[8,128,128]{2,1,0:T(8,128)} %diag_hbm.1) | copy-start | bytes 1572868
  4.3 0.7 copy-start.3
  4.9 0.7 copy-start.4
  5.6 0.7 copy-start.5

commit v3 on v2

--- a/solution.py
+++ b/solution.py
@@ -54,13 +54,12 @@
 
 def kernel(
     n,
-    pattern,
-    pattern_rows,
-    counts,
-    samples,
+    pattern_hbm,
+    counts_hbm,
+    samples_hbm,
     diag_hbm,
     off_hbm,
-    term,
+    term_hbm,
     diag_out,
     off_out,
     objective,
@@ -78,6 +77,11 @@
     logs,
     table_rows,
     table_smem,
+    pattern,
+    pattern_rows,
+    counts,
+    samples,
+    term,
     load_sems,
     out_sems,
     x_send_sems,
@@ -93,11 +97,35 @@
     columns = samples.shape[2]
     width = 2.0 * columns
 
+    def load(source, target, which):
+        copy = pltpu.make_async_copy(source, target, load_sems.at[which])
+        copy.start()
+        return copy
+
+    load_pattern_rows = load(pattern_hbm, pattern_rows, 3)
+    load_pattern = load(pattern_hbm, pattern, 4)
+    load_samples = load(samples_hbm, samples, 5)
+    load_counts = load(counts_hbm, counts, 6)
+    load_term = load(term_hbm, term, 7)
     load_diag = pltpu.make_async_copy(diag_hbm, diag, load_sems.at[0])
     load_off = pltpu.make_async_copy(off_hbm, off, load_sems.at[1])
     load_diag.start()
     load_off.start()
 
+    barrier = pltpu.get_barrier_semaphore()
+
+    def greet(i, carry):
+        pl.semaphore_signal(
+            barrier,
+            inc=1,
+            device_id={AXIS: peer_of(me, n - 1 - i, n)},
+            device_id_type=pl.DeviceIdType.MESH,
+        )
+        return carry
+
+    lax.fori_loop(0, n - 1, greet, 0)
+
+    load_pattern_rows.wait()
     row, col = pattern_rows[0:1, :], pattern_rows[1:2, :]
     blocks = rows * n
     forth, back, top = row * blocks + col, col * blocks + row, blocks * blocks
@@ -120,19 +148,6 @@
     def find(which, peer):
         return table_smem[peer, which] % entries
 
-    barrier = pltpu.get_barrier_semaphore()
-
-    def greet(i, carry):
-        pl.semaphore_signal(
-            barrier,
-            inc=1,
-            device_id={AXIS: peer_of(me, n - 1 - i, n)},
-            device_id_type=pl.DeviceIdType.MESH,
-        )
-        return carry
-
-    lax.fori_loop(0, n - 1, greet, 0)
-
     def remote(source, target, send_sems, recv_sems, peer, mine):
         return pltpu.make_async_remote_copy(
             src_ref=source.at[peer],
@@ -149,6 +164,8 @@
         remote, aux_send, aux_recv, aux_send_sems, aux_recv_sems
     )
 
+    load_pattern.wait()
+    load_samples.wait()
     load_table.wait()
     pl.semaphore_wait(barrier, n - 1)
 
@@ -167,6 +184,7 @@
     )
     identity = eye.astype(jnp.float32)
 
+    load_counts.wait()
     total = jnp.int32(0)
     for r in range(rows):
         count = counts[r]
@@ -187,7 +205,7 @@
     load_off.wait()
 
     def take_samples(i, carry):
-        peer = peer_of(me, n - 1 - i, n)
+        peer = peer_of(me, i + 1, n)
         x_copy(peer, peer).wait_recv()
         for slot in range(2):
             entry = find(2 + slot, peer)
@@ -249,10 +267,11 @@
         diag_out[r] = jnp.where(eye, moved, soften(moved, STEP_SIZE * PENALTY))
         return carry
 
+    load_term.wait()
     lax.fori_loop(0, rows, finish_diag, 0)
 
     def take_products(i, carry):
-        peer = peer_of(me, n - 1 - i, n)
+        peer = peer_of(me, i + 1, n)
         aux_copy(peer, peer).wait_recv()
         q_copy(peer, peer).wait_recv()
         for slot in range(2):
@@ -315,7 +334,6 @@
     columns = samples.shape[1]
     entries = omega_off.shape[0]
     f32, bf16, i16 = jnp.float32, jnp.bfloat16, jnp.int16
-    smem = pl.BlockSpec(memory_space=pltpu.SMEM)
     vmem = pl.BlockSpec(memory_space=pltpu.VMEM)
     hbm = pl.BlockSpec(memory_space=pl.ANY)
     dma = pltpu.SemaphoreType.DMA
@@ -330,7 +348,7 @@
             jax.ShapeDtypeStruct(omega_off.shape, f32),
             jax.ShapeDtypeStruct((1, edge), f32),
         ),
-        in_specs=[smem, vmem, smem, vmem, hbm, hbm, vmem],
+        in_specs=[pl.BlockSpec(memory_space=pltpu.HBM)] * 6,
         out_specs=(vmem, hbm, vmem),
         scratch_shapes=[
             pltpu.VMEM(omega_diag.shape, f32),
@@ -347,7 +365,12 @@
             pltpu.VMEM((1, edge), f32),
             pltpu.VMEM((n, 128), jnp.int32),
             pltpu.SMEM((n, 128), jnp.int32),
-            dma((3,)),
+            pltpu.SMEM((2, entries), jnp.int32),
+            pltpu.VMEM((2, entries), jnp.int32),
+            pltpu.SMEM((rows,), jnp.int32),
+            pltpu.VMEM((rows, edge, columns), bf16),
+            pltpu.VMEM((rows, edge), f32),
+            dma((8,)),
             dma((entries,)),
         ]
         + [dma((n,))] * 6,
@@ -357,13 +380,17 @@
             vmem_limit_bytes=min(held + (4 << 20), 60 << 20),
         ),
     )(
-        pattern.T,
-        pattern.T,
-        block_count,
-        samples.reshape(rows, edge, columns),
-        omega_diag,
-        omega_off,
-        diag_term.reshape(rows, edge),
+        *(
+            pltpu.with_memory_space_constraint(value, pltpu.HBM)
+            for value in (
+                pattern.T,
+                block_count,
+                samples.reshape(rows, edge, columns),
+                omega_diag,
+                omega_off,
+                diag_term.reshape(rows, edge),
+            )
+        )
     )
     return diag_next, off_next, objective[0, :1]
 

time: 96 us -> 89.3 us (0.930)
  local copies, waits for them, and re-layouts: 7.71 us -> 2.07 us
  Pallas kernels: 86.2 us -> 85.2 us
    unnamed x14 -> x2, local copies, waits for them, and re-layouts: 7.71 us -> 2.07 us
    pallas_call x1, Pallas kernels: 86.2 us -> 85.2 us  [shards(): pl.pallas_call(functools.partial(kernel, n), out_shape=(jax.ShapeDtypeStr...]
where the time goes in v3:
time: 89.3 us; the launch traced here: 89.1 us
  Pallas kernels  85.2 us (95%)
  local copies, waits for them, and re-layouts  2.07 us (2%)
  between operations  1.81 us (2%)
    pallas_call x1, Pallas kernels, shards(): pl.pallas_call(functools.partial(kernel, n), out_shape=(jax.ShapeDtypeStr...  85.2 us
    unnamed x2, local copies, waits for them, and re-layouts  2.07 us

profile of v3, /device:TPU:0, one launch (start us, length us, event | category | flops | bytes accessed | tf_op | source)
XLA Modules:
  0.0 89.1 jit_solution(10333195494690173069)
XLA Ops:
  0.6 85.2 %shard_map.85 = (f32[8,128,128]{2,1,0:T(8,128)S(1)}, f32[30,128,128]{2,1,0:T(8,128)S(1)}, f32[1,128]{1,0:T(1,128)S(1)}) custom-call(s32[2,30]{1,0:T(2,128)} %bitcast.8, s32[8]{0:T(128)} %counts_hbm.1, bf16[8,128,256]{2,1,0:T(8,128)(2,1)} %bitcast.6, f32[8,128,128]{2,1,0:T(8,128)} %diag_hbm.1, f32[30,128,128]{2,1,0:T(8,128)} %off_hbm.1, f32[8,128]{1,0:T(8,128)} %bitcast.7), custom_call_target="tpu_custom_call" | custom-call | tf_op jit(solution)/shard_map/pallas_call | solution.py:344
  85.9 0.8 copy.12
  86.7 1.3 %copy.13 = f32[30,128,128]{2,1,0:T(8,128)} copy(f32[30,128,128]{2,1,0:T(8,128)S(1)} %get-tuple-element.13) | data formatting | bytes 3932160

commit v4 on v3

--- a/solution.py
+++ b/solution.py
@@ -50,6 +50,11 @@
         total = total + bit * (((me // bit) % 2 + (step // bit) % 2) % 2)
         bit *= 2
     return total
+
+
+def spread(i, n):
+    half, odd = (i + 1) // 2, i % 2
+    return odd * half + (1 - odd) * (n - 1 - half)
 
 
 def kernel(
@@ -118,7 +123,7 @@
         pl.semaphore_signal(
             barrier,
             inc=1,
-            device_id={AXIS: peer_of(me, n - 1 - i, n)},
+            device_id={AXIS: peer_of(me, spread(i, n), n)},
             device_id_type=pl.DeviceIdType.MESH,
         )
         return carry
@@ -170,7 +175,7 @@
     pl.semaphore_wait(barrier, n - 1)
 
     def send_samples(i, carry):
-        peer = peer_of(me, n - 1 - i, n)
+        peer = peer_of(me, spread(i, n), n)
         for slot in range(2):
             entry = find(slot, peer)
             x_send[peer, slot] = samples[pattern[0, entry] % rows]
@@ -205,7 +210,7 @@
     load_off.wait()
 
     def take_samples(i, carry):
-        peer = peer_of(me, i + 1, n)
+        peer = peer_of(me, spread(i, n), n)
         x_copy(peer, peer).wait_recv()
         for slot in range(2):
             entry = find(2 + slot, peer)
@@ -240,7 +245,7 @@
     aux_recv[me, 2:3, :] = lanes
 
     def send_products(i, carry):
-        peer = peer_of(me, n - 1 - i, n)
+        peer = peer_of(me, spread(i, n), n)
         for slot in range(2):
             entry = find(slot, peer)
             values = runs[last[pattern[0, entry] % rows]]
@@ -271,7 +276,7 @@
     lax.fori_loop(0, rows, finish_diag, 0)
 
     def take_products(i, carry):
-        peer = peer_of(me, i + 1, n)
+        peer = peer_of(me, spread(i, n), n)
         aux_copy(peer, peer).wait_recv()
         q_copy(peer, peer).wait_recv()
         for slot in range(2):
@@ -313,7 +318,7 @@
     )
 
     def drain(i, carry):
-        peer = peer_of(me, n - 1 - i, n)
+        peer = peer_of(me, spread(i, n), n)
         x_copy(peer, me).wait_send()
         q_copy(peer, me).wait_send()
         aux_copy(peer, me).wait_send()

time: 89.3 us -> 85.2 us (0.954)
  Pallas kernels: 85.2 us -> 81.2 us
    pallas_call x1, Pallas kernels: 85.2 us -> 81.2 us  [shards(): pl.pallas_call(functools.partial(kernel, n), out_shape=(jax.ShapeDtypeStr...]
where the time goes in v4:
time: 85.2 us; the launch traced here: 85 us
  Pallas kernels  81.2 us (95%)
  local copies, waits for them, and re-layouts  2.07 us (2%)
  between operations  1.81 us (2%)
    pallas_call x1, Pallas kernels, shards(): pl.pallas_call(functools.partial(kernel, n), out_shape=(jax.ShapeDtypeStr...  81.2 us
    unnamed x2, local copies, waits for them, and re-layouts  2.07 us

profile of v4, /device:TPU:0, one launch (start us, length us, event | category | flops | bytes accessed | tf_op | source)
XLA Modules:
  0.0 85.0 jit_solution(18360279201598935961)
XLA Ops:
  0.6 81.2 %shard_map.85 = (f32[8,128,128]{2,1,0:T(8,128)S(1)}, f32[30,128,128]{2,1,0:T(8,128)S(1)}, f32[1,128]{1,0:T(1,128)S(1)}) custom-call(s32[2,30]{1,0:T(2,128)} %bitcast.8, s32[8]{0:T(128)} %counts_hbm.1, bf16[8,128,256]{2,1,0:T(8,128)(2,1)} %bitcast.6, f32[8,128,128]{2,1,0:T(8,128)} %diag_hbm.1, f32[30,128,128]{2,1,0:T(8,128)} %off_hbm.1, f32[8,128]{1,0:T(8,128)} %bitcast.7), custom_call_target="tpu_custom_call" | custom-call | tf_op jit(solution)/shard_map/pallas_call | solution.py:349
  81.8 0.8 copy.12
  82.6 1.3 %copy.13 = f32[30,128,128]{2,1,0:T(8,128)} copy(f32[30,128,128]{2,1,0:T(8,128)S(1)} %get-tuple-element.13) | data formatting | bytes 3932160

commit v5 on v4

--- a/solution.py
+++ b/solution.py
@@ -123,7 +123,7 @@
         pl.semaphore_signal(
             barrier,
             inc=1,
-            device_id={AXIS: peer_of(me, spread(i, n), n)},
+            device_id={AXIS: peer_of(me, spread((i + me % 2) % (n - 1), n), n)},
             device_id_type=pl.DeviceIdType.MESH,
         )
         return carry
@@ -175,7 +175,7 @@
     pl.semaphore_wait(barrier, n - 1)
 
     def send_samples(i, carry):
-        peer = peer_of(me, spread(i, n), n)
+        peer = peer_of(me, spread((i + me % 2) % (n - 1), n), n)
         for slot in range(2):
             entry = find(slot, peer)
             x_send[peer, slot] = samples[pattern[0, entry] % rows]
@@ -210,7 +210,7 @@
     load_off.wait()
 
     def take_samples(i, carry):
-        peer = peer_of(me, spread(i, n), n)
+        peer = peer_of(me, spread((i + me % 2) % (n - 1), n), n)
         x_copy(peer, peer).wait_recv()
         for slot in range(2):
             entry = find(2 + slot, peer)
@@ -245,7 +245,7 @@
     aux_recv[me, 2:3, :] = lanes
 
     def send_products(i, carry):
-        peer = peer_of(me, spread(i, n), n)
+        peer = peer_of(me, spread((i + me % 2) % (n - 1), n), n)
         for slot in range(2):
             entry = find(slot, peer)
             values = runs[last[pattern[0, entry] % rows]]
@@ -276,7 +276,7 @@
     lax.fori_loop(0, rows, finish_diag, 0)
 
     def take_products(i, carry):
-        peer = peer_of(me, spread(i, n), n)
+        peer = peer_of(me, spread((i + me % 2) % (n - 1), n), n)
         aux_copy(peer, peer).wait_recv()
         q_copy(peer, peer).wait_recv()
         for slot in range(2):
@@ -318,7 +318,7 @@
     )
 
     def drain(i, carry):
-        peer = peer_of(me, spread(i, n), n)
+        peer = peer_of(me, spread((i + me % 2) % (n - 1), n), n)
         x_copy(peer, me).wait_send()
         q_copy(peer, me).wait_send()
         aux_copy(peer, me).wait_send()

time: 85.2 us -> 85.5 us (level)
  no operation moved by 1% of the time
where the time goes in v5:
time: 85.5 us; the launch traced here: 85.4 us
  Pallas kernels  81.5 us (95%)
  local copies, waits for them, and re-layouts  2.07 us (2%)
  between operations  1.81 us (2%)
    pallas_call x1, Pallas kernels, shards(): pl.pallas_call(functools.partial(kernel, n), out_shape=(jax.ShapeDtypeStr...  81.5 us
    unnamed x2, local copies, waits for them, and re-layouts  2.07 us

profile of v5, /device:TPU:0, one launch (start us, length us, event | category | flops | bytes accessed | tf_op | source)
XLA Modules:
  0.0 85.4 jit_solution(5340516132050844425)
XLA Ops:
  0.6 81.5 %shard_map.85 = (f32[8,128,128]{2,1,0:T(8,128)S(1)}, f32[30,128,128]{2,1,0:T(8,128)S(1)}, f32[1,128]{1,0:T(1,128)S(1)}) custom-call(s32[2,30]{1,0:T(2,128)} %bitcast.8, s32[8]{0:T(128)} %counts_hbm.1, bf16[8,128,256]{2,1,0:T(8,128)(2,1)} %bitcast.6, f32[8,128,128]{2,1,0:T(8,128)} %diag_hbm.1, f32[30,128,128]{2,1,0:T(8,128)} %off_hbm.1, f32[8,128]{1,0:T(8,128)} %bitcast.7), custom_call_target="tpu_custom_call" | custom-call | tf_op jit(solution)/shard_map/pallas_call | solution.py:349
  82.1 0.8 copy.12
  82.9 1.3 %copy.13 = f32[30,128,128]{2,1,0:T(8,128)} copy(f32[30,128,128]{2,1,0:T(8,128)S(1)} %get-tuple-element.13) | data formatting | bytes 3932160
